TPU v7x, 32 devices: a whole 2x2x4 slice. The times are simulated.
32 devices in a mesh: parts: 2 (over x), aux: 16 (over z, y, core).
Axes of the slice: x: 2, y: 2, z: 4, core: 2. Of those that a mesh axis runs over, the one named last changes fastest.
Arguments:
- tiles: bfloat16 [32, 8, 8, 128, 128], P(('parts', 'aux')), parts along dimension 0, may hold values from -6 to 6
- mu_list: int32 [32, 8], P(('parts', 'aux')), parts along dimension 0, may hold values from 0 to 7
- lam_list: int32 [32, 8], P(('parts', 'aux')), parts along dimension 0, may hold values from 0 to 7
- tile_count: int32 [32], P(('parts', 'aux')), parts along dimension 0, may hold values from 1 to 8, as said below
- coeff: bfloat16 [2048, 256], P(('parts', 'aux')), parts along dimension 0, may hold values from -0.5 to 0.5
- owner: int32 [32], P('parts'), parts along dimension 0, may hold values from 0 to 15, each once
Outputs:
- exchange: float32 [2048, 1024], P(('parts', 'aux')), parts along dimension 0
There are 2 independent parts, one for each index of `parts`. A program takes and returns all parts, laid end to end along the dimension named above; each array names one. Nothing has to cross between parts.
Inputs may be any that keep to these rules, and one draw needn't show every extreme that they name: Slots from tile_count on are padding and are ignored; in every draw some shard uses all 8 slots.
All inputs are finite; a program needn't handle non-finite values.
Results may differ from a plain program's by a relative error of at most 0.00088.
Values may be sent and summed in bfloat16 or wider, within the bound.
A program may use at most 64 MiB of HBM per device.

v0:
```python
import jax
import jax.numpy as jnp
from jax import lax
from jax.sharding import PartitionSpec as P


def body(tiles, mu_list, lam_list, tile_count, coeff, owner):
    shards = lax.axis_size("aux")
    whole_coeff = lax.all_gather(coeff, "aux", axis=0, tiled=True)
    nbasis, occupied = whole_coeff.shape
    slots = tiles.shape[1]
    aux_local = tiles.shape[2]
    block = tiles.shape[3]
    nblocks = nbasis // block
    tile_rows = nbasis // shards
    picked = whole_coeff.reshape(nblocks, block, occupied)[lam_list[0]]
    live = (jnp.arange(slots) < tile_count[0]).astype(jnp.float32)
    products = jnp.einsum("tpml,tlo->tpmo", tiles[0], picked, preferred_element_type=jnp.float32)
    placing = (mu_list[0][:, None] == jnp.arange(nblocks)[None, :]).astype(jnp.float32) * live[
        :, None
    ]
    half_form = jnp.einsum(
        "tb,tpmo->pbmo", placing, products, precision=lax.Precision.HIGHEST
    ).astype(jnp.bfloat16)
    ordered = half_form.reshape(aux_local, shards, tile_rows, occupied)[:, owner].reshape(
        aux_local, nbasis, occupied
    )
    scale = 1.0 / (aux_local * shards * occupied)
    summed = lax.psum_scatter(
        jnp.einsum("prk,psk->rs", ordered, ordered, preferred_element_type=jnp.float32),
        "aux",
        scatter_dimension=0,
        tiled=True,
    )
    return summed * scale


def solution(mesh):
    return jax.shard_map(
        body,
        mesh=mesh,
        in_specs=(
            P(("parts", "aux"), None, None, None, None),
            P(("parts", "aux"), None),
            P(("parts", "aux"), None),
            P(("parts", "aux")),
            P(("parts", "aux"), None),
            P("parts"),
        ),
        out_specs=P(("parts", "aux"), None),
        check_vma=False,
    )
```

profile of v0, /device:TPU:0, one launch (start us, length us, event | category | flops | bytes accessed | tf_op | source)
XLA Modules:
  0.0 151.5 jit_solution(12048981923072878204)
XLA Ops:
  6.5 0.0 copy-start
  6.5 0.0 reduce-scatter.2.cloned.1.call-start
  6.5 24.9 %all_gather.3 = bf16[1024,256]{1,0:T(8,128)(2,1)S(1)} all-gather(bf16[64,256]{1,0:T(8,128)(2,1)} %param.10), channel_id=1, replica_groups=mesh['parts'=2,'aux'=16] {'aux'}, dimensions={0}, use_global_device_ids=true | all-gather | bytes 557056 | tf_op jit(solution)/shard_map/all_gather | solution.py:9
  31.4 0.7 fusion.7
  32.1 0.6 gather_fusion
  32.7 0.0 copy-done
  32.7 4.5 %convolution_bitcast_fusion = f32[8,8,128,256]{2,3,1,0:T(8,128)} fusion(bf16[1,8,8,128,128]{4,3,2,1,0:T(8,128)(2,1)S(1)} %copy-done, bf16[8,128,256]{2,1,0:T(8,128)(2,1)S(1)} %gather_fusion), kind=kOutput, calls=%fused_computation.3 | convolution fusion | flops 536870912 | bytes 11010048 | tf_op jit(solution)/shard_map/tpml,tlo->tpmo/dot_general | solution.py:18
  37.2 0.0 copy-start.1
  37.2 9.2 %copy.12 = f32[8,8,128,256]{3,0,2,1:T(8,128)} copy(f32[8,8,128,256]{2,3,1,0:T(8,128)} %convolution_bitcast_fusion) | data formatting | bytes 16777216 | tf_op jit(solution)/shard_map/tpml,tlo->tpmo/dot_general | solution.py:18
  47.1 0.0 copy-done.1
  47.1 9.4 %convert_bitcast_fusion = bf16[8,8,128,256]{3,1,2,0:T(8,128)(2,1)S(1)} fusion(f32[8,8,128,256]{3,0,2,1:T(8,128)} %copy.12, f32[8]{0:T(128)S(1)} %compare_convert_fusion, s32[8]{0:T(128)S(1)} %bitcast.37), kind=kOutput, calls=%fused_computation.2 | convolution fusion | flops 203423872 | bytes 12582976 | tf_op jit(solution)/shard_map/tb,tpmo->pbmo/dot_general | solution.py:22
  56.6 0.0 copy-start.2
  56.6 3.0 %copy.13 = bf16[8,8,128,256]{3,2,1,0:T(8,128)(2,1)} copy(bf16[8,8,128,256]{3,1,2,0:T(8,128)(2,1)S(1)} %convert_bitcast_fusion) | data formatting | bytes 8388608 | tf_op jit(solution)/shard_map/convert_element_type | solution.py:24
  59.6 0.0 copy-done.2
  59.6 5.0 %gather_fusion.1 = bf16[16,8,64,256]{3,2,1,0:T(8,128)(2,1)} fusion(bf16[8,16,64,256]{3,2,1,0:T(8,128)(2,1)} %bitcast.33, s32[1024]{0:T(1024)S(1)} %pad_clamp_fusion), kind=kCustom, calls=%fused_computation.1 | custom fusion | bytes 8388672 | tf_op jit(solution)/shard_map/gather | solution.py:25
  64.6 2.5 %copy.14 = bf16[8,16,64,256]{3,2,1,0:T(8,128)(2,1)S(1)} copy(bf16[8,16,64,256]{3,2,0,1:T(8,128)(2,1)} %bitcast.34) | data formatting | bytes 8388608 | tf_op jit(solution)/shard_map/gather | solution.py:25
  67.1 6.1 %convolution_bitcast_fusion.1 = f32[1024,1024]{1,0:T(8,128)} fusion(bf16[8,1024,256]{2,1,0:T(8,128)(2,1)S(1)} %bitcast.35), kind=kOutput, calls=%fused_computation.4 | convolution fusion | flops 4294967296 | bytes 8388608 | tf_op jit(solution)/shard_map/prk,psk->rs/dot_general | solution.py:30
  73.2 0.0 reduce-scatter.2.cloned.1.call-update
  73.2 69.8 %reduce-scatter.2.cloned.1.call-done = f32[64,1024]{1,0:T(8,128)} async-done(((f32[1024,1024]{1,0:T(8,128)}), f32[64,1024]{1,0:T(8,128)}) %reduce-scatter.2.cloned.1.call-update) | async-done | bytes 262160 | tf_op jit(solution)/shard_map/reduce_scatter | solution.py:29
  143.0 1.7 %broadcast_multiply_fusion = f32[64,1024]{1,0:T(8,128)} fusion(f32[64,1024]{1,0:T(8,128)} %reduce-scatter.2.cloned.1.call-done), kind=kLoop, calls=%fused_computation.7 | loop fusion | flops 65536 | bytes 524288 | tf_op jit(solution)/shard_map/mul | solution.py:35
  (4 shorter events, 0.0 us)
Async XLA Ops:
  6.5 26.2 %copy-start = (bf16[1,8,8,128,128]{4,3,2,1,0:T(8,128)(2,1)S(1)}, bf16[1,8,8,128,128]{4,3,2,1,0:T(8,128)(2,1)}, u32[]{:S(2)}) copy-start(bf16[1,8,8,128,128]{4,3,2,1,0:T(8,128)(2,1)} %param.6) | copy-start | bytes 6291460
  6.5 136.5 %reduce-scatter.2.cloned.1.call-start = ((), (), s32[]{:S(2)}) async-start(), calls=%async_computation.1 | async-start | bytes 4456448 | tf_op jit(solution)/shard_map/reduce_scatter | solution.py:29
  37.2 9.9 %copy-start.1 = (s32[1,8]{1,0:T(1,128)S(1)}, s32[1,8]{1,0:T(1,128)}, u32[]{:S(2)}) copy-start(s32[1,8]{1,0:T(1,128)} %param.7) | copy-start | bytes 100
  56.6 3.0 %copy-start.2 = (s32[16]{0:T(128)S(1)}, s32[16]{0:T(128)}, u32[]{:S(2)}) copy-start(s32[16]{0:T(128)} %param.11) | copy-start | bytes 196
Sparse Core Ops, SparseCore 0:
  73.3 69.6 reduce-scatter.1
where the time goes:
time: 152 us
  waiting for transfers between devices  69.8 us (46%)
  blocking collectives  24.9 us (16%)
  local copies, waits for them, and re-layouts  20.3 us (13%)
  matrix products  20.1 us (13%)
  between operations  14.1 us (9%)
  other arithmetic  2.35 us (2%)
    reduce_scatter x1, waiting for transfers between devices, body(): lax.psum_scatter(jnp.einsum('prk,psk->rs', ordered, ordered, preferred_el...  69.8 us
    all_gather x1, blocking collectives, body(): whole_coeff = lax.all_gather(coeff, 'aux', axis=0, tiled=True)  24.9 us
    dot_general x1, matrix products, body(): jnp.einsum('tb,tpmo->pbmo', placing, products, precision=lax.Precision.HI...  9.44 us
    dot_general x1, local copies, waits for them, and re-layouts, body(): jnp.einsum('tpml,tlo->tpmo', tiles[0], picked, preferred_element_type=jnp...  9.21 us
    gather x2, local copies, waits for them, and re-layouts, body(): half_form.reshape(aux_local, shards, tile_rows, occupied)[:, owner]  7.47 us
    dot_general x1, matrix products, body(): jnp.einsum('prk,psk->rs', ordered, ordered, preferred_element_type=jnp.fl...  6.09 us
    dot_general x1, matrix products, body(): jnp.einsum('tpml,tlo->tpmo', tiles[0], picked, preferred_element_type=jnp...  4.52 us
  transfers between devices with their start and end apart: 1, of which 1 were waited for; matrix products, arithmetic and copies ran while one was open for 0% of the time, Pallas kernels for 0%

commit v1 on v0

--- a/solution.py
+++ b/solution.py
@@ -6,7 +6,9 @@
 
 def body(tiles, mu_list, lam_list, tile_count, coeff, owner):
     shards = lax.axis_size("aux")
-    whole_coeff = lax.all_gather(coeff, "aux", axis=0, tiled=True)
+    res = jnp.stack([coeff for _ in range(jax.lax.axis_size("aux"))], axis=0)
+    fresh = jax.lax.all_to_all(res, axis_name="aux", split_axis=0, concat_axis=0)
+    whole_coeff = jnp.concatenate(fresh, axis=0)
     nbasis, occupied = whole_coeff.shape
     slots = tiles.shape[1]
     aux_local = tiles.shape[2]

time: 152 us -> 152 us (level)
  blocking collectives: 24.9 us -> 0 us
  waiting for transfers between devices: 69.8 us -> 84.7 us
  starting transfers between devices: 0.01 us -> 7.43 us
  local copies, waits for them, and re-layouts: 20.3 us -> 22 us
    all_gather x1 -> x0, blocking collectives: 24.9 us -> none  [body(): whole_coeff = lax.all_gather(coeff, 'aux', axis=0, tiled=True)]
    all_to_all x0 -> x1, waiting for transfers between devices: none -> 12.4 us  [body(): jax.lax.all_to_all(res, axis_name='aux', split_axis=0, concat_axis=0)]
    all_to_all x0 -> x1, starting transfers between devices: none -> 7.39 us  [body(): jax.lax.all_to_all(res, axis_name='aux', split_axis=0, concat_axis=0)]
    reduce_scatter x1, waiting for transfers between devices: 69.8 us -> 72.3 us  [body(): lax.psum_scatter(jnp.einsum('prk,psk->rs', ordered, ordered, preferred_el...]
    another operation x0 -> x1, local copies, waits for them, and re-layouts: none -> 1.75 us  [body(): res = jnp.stack([coeff for _ in range(jax.lax.axis_size('aux'))], axis=0)]
  transfers between devices with their start and end apart: 1 -> 2, of which waited for: 1 -> 2; matrix products, arithmetic and copies ran while one was open for 0% -> 1% of each run, Pallas kernels for 0% -> 0%
where the time goes in v1:
time: 152 us; the launch traced here: 151 us
  waiting for transfers between devices  84.7 us (56%)
  local copies, waits for them, and re-layouts  22 us (14%)
  matrix products  20 us (13%)
  between operations  14.1 us (9%)
  starting transfers between devices  7.43 us (5%)
  other arithmetic  3.01 us (2%)
    reduce_scatter x1, waiting for transfers between devices, body(): lax.psum_scatter(jnp.einsum('prk,psk->rs', ordered, ordered, preferred_el...  72.3 us
    all_to_all x1, waiting for transfers between devices, body(): jax.lax.all_to_all(res, axis_name='aux', split_axis=0, concat_axis=0)  12.4 us
    dot_general x1, matrix products, body(): jnp.einsum('tb,tpmo->pbmo', placing, products, precision=lax.Precision.HI...  9.43 us
    dot_general x1, local copies, waits for them, and re-layouts, body(): jnp.einsum('tpml,tlo->tpmo', tiles[0], picked, preferred_element_type=jnp...  9.21 us
    gather x2, local copies, waits for them, and re-layouts, body(): half_form.reshape(aux_local, shards, tile_rows, occupied)[:, owner]  7.46 us
    all_to_all x1, starting transfers between devices, body(): jax.lax.all_to_all(res, axis_name='aux', split_axis=0, concat_axis=0)  7.39 us
    dot_general x1, matrix products, body(): jnp.einsum('prk,psk->rs', ordered, ordered, preferred_element_type=jnp.fl...  6.08 us
    dot_general x1, matrix products, body(): jnp.einsum('tpml,tlo->tpmo', tiles[0], picked, preferred_element_type=jnp...  4.51 us
  transfers between devices with their start and end apart: 2, of which 2 were waited for; matrix products, arithmetic and copies ran while one was open for 1% of the time, Pallas kernels for 0%

profile of v1, /device:TPU:0, one launch (start us, length us, event | category | flops | bytes accessed | tf_op | source)
XLA Modules:
  0.0 151.3 jit_solution(17203938971172059097)
XLA Ops:
  6.5 0.0 copy-start
  6.5 1.8 %stack.2 = bf16[16,64,256]{2,1,0:T(8,128)(2,1)} broadcast(bf16[64,256]{1,0:T(8,128)(2,1)} %param.10), dimensions={1,2} | broadcast | bytes 557056 | tf_op jit(solution)/shard_map/stack | solution.py:9
  8.3 7.4 %all-to-all-start = ((bf16[16,64,256]{2,1,0:T(8,128)(2,1)}), bf16[16,64,256]{2,1,0:T(8,128)(2,1)S(1)}, u32[]{:S(2)}, u32[]{:S(2)}) async-start(bf16[16,64,256]{2,1,0:T(8,128)(2,1)} %stack.2), calls=%async_computation | async-start | bytes 1048576 | tf_op jit(solution)/shard_map/all_to_all | solution.py:10
  15.7 0.0 reduce-scatter.2.cloned.1.call-start
  16.4 0.7 fusion.7
  17.1 0.7 compare_select_fusion
  17.7 12.4 %all-to-all-done = bf16[16,64,256]{2,1,0:T(8,128)(2,1)S(1)} async-done(((bf16[16,64,256]{2,1,0:T(8,128)(2,1)}), bf16[16,64,256]{2,1,0:T(8,128)(2,1)S(1)}, u32[]{:S(2)}, u32[]{:S(2)}) %all-to-all-start) | async-done | bytes 524320 | tf_op jit(solution)/shard_map/all_to_all | solution.py:10
  30.2 0.6 gather_fusion
  30.7 0.0 copy-done
  30.8 4.5 %convolution_bitcast_fusion = f32[8,8,128,256]{2,3,1,0:T(8,128)} fusion(bf16[1,8,8,128,128]{4,3,2,1,0:T(8,128)(2,1)S(1)} %copy-done, bf16[8,128,256]{2,1,0:T(8,128)(2,1)S(1)} %gather_fusion), kind=kOutput, calls=%fused_computation.3 | convolution fusion | flops 536870912 | bytes 11010048 | tf_op jit(solution)/shard_map/tpml,tlo->tpmo/dot_general | solution.py:20
  35.3 0.0 copy-start.1
  35.3 9.2 %copy.12 = f32[8,8,128,256]{3,0,2,1:T(8,128)} copy(f32[8,8,128,256]{2,3,1,0:T(8,128)} %convolution_bitcast_fusion) | data formatting | bytes 16777216 | tf_op jit(solution)/shard_map/tpml,tlo->tpmo/dot_general | solution.py:20
  44.5 0.0 copy-done.1
  44.5 9.4 %convert_bitcast_fusion = bf16[8,8,128,256]{3,1,2,0:T(8,128)(2,1)S(1)} fusion(f32[8,8,128,256]{3,0,2,1:T(8,128)} %copy.12, f32[8]{0:T(128)S(1)} %compare_convert_fusion, s32[8]{0:T(128)S(1)} %bitcast.37), kind=kOutput, calls=%fused_computation.2 | convolution fusion | flops 203423872 | bytes 12582976 | tf_op jit(solution)/shard_map/tb,tpmo->pbmo/dot_general | solution.py:24
  53.9 3.0 %copy.13 = bf16[8,8,128,256]{3,2,1,0:T(8,128)(2,1)} copy(bf16[8,8,128,256]{3,1,2,0:T(8,128)(2,1)S(1)} %convert_bitcast_fusion) | data formatting | bytes 8388608 | tf_op jit(solution)/shard_map/convert_element_type | solution.py:26
  56.9 5.0 %gather_fusion.1 = bf16[16,8,64,256]{3,2,1,0:T(8,128)(2,1)} fusion(bf16[8,16,64,256]{3,2,1,0:T(8,128)(2,1)} %bitcast.33, s32[1024]{0:T(1024)S(1)} %pad_clamp_fusion), kind=kCustom, calls=%fused_computation.1 | custom fusion | bytes 8388672 | tf_op jit(solution)/shard_map/gather | solution.py:27
  61.9 2.5 %copy.14 = bf16[8,16,64,256]{3,2,1,0:T(8,128)(2,1)S(1)} copy(bf16[8,16,64,256]{3,2,0,1:T(8,128)(2,1)} %bitcast.34) | data formatting | bytes 8388608 | tf_op jit(solution)/shard_map/gather | solution.py:27
  64.4 6.1 %convolution_bitcast_fusion.1 = f32[1024,1024]{1,0:T(8,128)} fusion(bf16[8,1024,256]{2,1,0:T(8,128)(2,1)S(1)} %bitcast.35), kind=kOutput, calls=%fused_computation.4 | convolution fusion | flops 4294967296 | bytes 8388608 | tf_op jit(solution)/shard_map/prk,psk->rs/dot_general | solution.py:32
  70.5 0.0 reduce-scatter.2.cloned.1.call-update
  70.5 72.3 %reduce-scatter.2.cloned.1.call-done = f32[64,1024]{1,0:T(8,128)} async-done(((f32[1024,1024]{1,0:T(8,128)}), f32[64,1024]{1,0:T(8,128)}) %reduce-scatter.2.cloned.1.call-update) | async-done | bytes 262160 | tf_op jit(solution)/shard_map/reduce_scatter | solution.py:31
  142.8 1.7 %broadcast_multiply_fusion = f32[64,1024]{1,0:T(8,128)} fusion(f32[64,1024]{1,0:T(8,128)} %reduce-scatter.2.cloned.1.call-done), kind=kLoop, calls=%fused_computation.7 | loop fusion | flops 65536 | bytes 524288 | tf_op jit(solution)/shard_map/mul | solution.py:37
  (3 shorter events, 0.0 us)
Async XLA Ops:
  6.5 24.2 %copy-start = (bf16[1,8,8,128,128]{4,3,2,1,0:T(8,128)(2,1)S(1)}, bf16[1,8,8,128,128]{4,3,2,1,0:T(8,128)(2,1)}, u32[]{:S(2)}) copy-start(bf16[1,8,8,128,128]{4,3,2,1,0:T(8,128)(2,1)} %param.6) | copy-start | bytes 6291460
  8.3 21.9 %all-to-all-start = ((bf16[16,64,256]{2,1,0:T(8,128)(2,1)}), bf16[16,64,256]{2,1,0:T(8,128)(2,1)S(1)}, u32[]{:S(2)}, u32[]{:S(2)}) async-start(bf16[16,64,256]{2,1,0:T(8,128)(2,1)} %stack.2), calls=%async_computation | async-start | bytes 1048576 | tf_op jit(solution)/shard_map/all_to_all | solution.py:10
  15.7 127.1 %reduce-scatter.2.cloned.1.call-start = ((), (), s32[]{:S(2)}) async-start(), calls=%async_computation.2 | async-start | bytes 4456448 | tf_op jit(solution)/shard_map/reduce_scatter | solution.py:31
  35.3 9.2 %copy-start.1 = (s32[1,8]{1,0:T(1,128)S(1)}, s32[1,8]{1,0:T(1,128)}, u32[]{:S(2)}) copy-start(s32[1,8]{1,0:T(1,128)} %param.7) | copy-start | bytes 100
Sparse Core Ops, SparseCore 0:
  70.6 72.1 reduce-scatter.1
